TPU v7x, 32 devices: a whole 2x2x4 slice. The times are simulated.
32 devices in a mesh: row: 8 (over z, x), layer: 4 (over y, core).
Axes of the slice: x: 2, y: 2, z: 4, core: 2. Of those that a mesh axis runs over, the one named last changes fastest.
Arguments:
- left_factor: float32 [4096, 512], P('row'), may hold values from -6 to 6
- right_factor: float32 [4096, 512], P(('row', 'layer')), may hold values from -0.25 to 0.25
- block_columns: int32 [32, 8], P('row', 'layer'), may hold values from -1 to 31, as said below
- labels: int32 [32, 8, 128, 128], P('row', 'layer'), may hold values 0 or 1
Outputs:
- left_grad: float32 [4096, 512], P('row', 'layer')
Inputs may be any that keep to these rules, and one draw needn't show every extreme that they name: `block_columns`: entries l*2 to (l+1)*2 - 1 of row t list, in ascending order and each once, occupied tile columns j of tile row t with j % 4 == l, then -1 in the unused slots; every list holds at least one column, and in every draw some list of each group l is full.
All inputs are finite; a program needn't handle non-finite values. No bound on the sum of `labels` on one device may be relied on, other than what follows from the above.
Results may differ from a plain program's by a relative error of at most 0.0003.
Values sent between devices are 32-bit elements; how exact they have to be, the bound alone decides.
A program may use at most 64 MiB of HBM per device.

v0:
```python
import jax
import jax.numpy as jnp
from jax import lax
from jax.sharding import PartitionSpec as P

shrink_rate = 0.1


def per_device(left_factor, right_factor, block_columns, labels):
    row_count = lax.axis_size("row")
    layer_count = lax.axis_size("layer")
    layer_index = lax.axis_index("layer")
    tile_size = right_factor.shape[0]
    tile_rows = block_columns.shape[0]
    gathered = lax.all_gather(right_factor, "row", axis=0, tiled=True)
    right_tiles = gathered.reshape(row_count, tile_size, -1)
    occupied = (block_columns >= 0).astype(jnp.float32)
    holder = jnp.clip(block_columns, 0, None) // layer_count
    picked = right_tiles[holder]
    left_tiles = left_factor.reshape(tile_rows, tile_size, -1)
    scores = jnp.einsum("tak,tsbk->tsab", left_tiles, picked, precision=lax.Precision.HIGHEST)
    residue = (jax.nn.sigmoid(scores) - labels.astype(jnp.float32)) * occupied[:, :, None, None]
    total = jnp.einsum("tsab,tsbk->tak", residue, picked, precision=lax.Precision.HIGHEST)
    total = total.reshape(left_factor.shape)
    shared = lax.psum_scatter(total, "layer", scatter_dimension=1, tiled=True)
    width = shared.shape[1]
    own_part = lax.dynamic_slice_in_dim(left_factor, layer_index * width, width, 1)
    return shared + shrink_rate * own_part


def solution(mesh):
    in_specs = (
        P("row", None),
        P(("row", "layer"), None),
        P("row", "layer"),
        P("row", "layer", None, None),
    )
    out_specs = P("row", "layer")
    return jax.shard_map(
        per_device, mesh=mesh, in_specs=in_specs, out_specs=out_specs, check_vma=False
    )
```

profile of v0, /device:TPU:0, one launch (start us, length us, event | category | flops | bytes accessed | tf_op | source)
XLA Modules:
  0.0 101.7 jit_solution(181040831652338331)
XLA Ops:
  6.5 0.0 all-gather.2.cloned.1.call-start
  6.5 0.7 all-gather.2.cloned.1.call-update
  7.3 0.0 reduce-scatter.2.cloned.1.call-start
  7.3 0.7 compare_select_fusion
  8.0 0.1 copy.7
  8.1 0.1 reshape.15
  8.2 0.7 compare_convert_fusion
  8.9 0.1 copy.8
  9.0 52.5 %all-gather.2.cloned.1.call-done = f32[1024,512]{1,0:T(8,128)} async-done(((f32[128,512]{1,0:T(8,128)}), f32[1024,512]{1,0:T(8,128)}) %all-gather.2.cloned.1.call-update) | async-done | bytes 2097168 | tf_op jit(solution)/shard_map/all_gather | solution.py:15
  61.5 0.0 copy-start
  61.5 2.4 %gather_fusion = f32[8,128,512]{2,1,0:T(8,128)S(1)} fusion(f32[8,128,512]{2,1,0:T(8,128)} %bitcast.24, s32[1024]{0:T(1024)S(1)} %pad_clamp_fusion), kind=kCustom, calls=%fused_computation | custom fusion | bytes 4194336 | tf_op jit(solution)/shard_map/gather | solution.py:19
  63.9 0.0 copy-done
  63.9 3.4 %fusion.5 = f32[4,2,128,128]{3,2,1,0:T(8,128)S(1)} fusion(f32[4,2,128,512]{3,2,1,0:T(8,128)S(1)} %bitcast.21, f32[4,128,512,1]{2,1,3,0:T(8,128)S(1)} %bitcast.25, s32[4,2,128,128]{3,2,1,0:T(8,128)} %param.7, f32[4,2]{1,0:T(4,128)S(1)} %copy.8), kind=kOutput, calls=%fused_computation.7 | convolution fusion | flops 806092800 | bytes 4194336 | tf_op jit(solution)/shard_map/tak,tsbk->tsab/dot_general | solution.py:21
  67.3 2.3 %fusion.6 = f32[4,128,512,1]{2,1,3,0:T(8,128)} fusion(f32[4,2,128,128]{3,2,1,0:T(8,128)S(1)} %fusion.5, f32[4,2,128,512]{3,2,1,0:T(8,128)S(1)} %bitcast.22), kind=kOutput, calls=%fused_computation.13 | convolution fusion | flops 805306368 | bytes 3670016 | tf_op jit(solution)/shard_map/tsab,tsbk->tak/dot_general | solution.py:23
  69.6 0.0 reduce-scatter.2.cloned.1.call-update
  69.6 23.5 %reduce-scatter.2.cloned.1.call-done = f32[512,128]{1,0:T(8,128)} async-done(((f32[512,512]{1,0:T(8,128)}), f32[512,128]{1,0:T(8,128)}) %reduce-scatter.2.cloned.1.call-update) | async-done | bytes 262160 | tf_op jit(solution)/shard_map/reduce_scatter | solution.py:25
  93.2 1.7 %multiply_add_fusion = f32[512,128]{1,0:T(8,128)} fusion(f32[512,128]{1,0:T(8,128)} %reduce-scatter.2.cloned.1.call-done, f32[512,512]{1,0:T(8,128)S(1)} %copy-done, s32[]{:T(128)S(6)} %select_n.13), kind=kLoop, calls=%fused_computation.8 | loop fusion | flops 131072 | bytes 786436 | tf_op jit(solution)/shard_map/add | solution.py:28
  (1 shorter events, 0.0 us)
Async XLA Ops:
  6.5 55.0 %all-gather.2.cloned.1.call-start = ((), (), s32[]{:S(2)}) async-start(), calls=%async_computation.1 | async-start | bytes 2359296 | tf_op jit(solution)/shard_map/all_gather | solution.py:15
  7.3 85.9 %reduce-scatter.2.cloned.1.call-start = ((), (), s32[]{:S(2)}) async-start(), calls=%async_computation.2 | async-start | bytes 1310720 | tf_op jit(solution)/shard_map/reduce_scatter | solution.py:25
  61.5 2.4 %copy-start = (f32[512,512]{1,0:T(8,128)S(1)}, f32[512,512]{1,0:T(8,128)}, u32[]{:S(2)}) copy-start(f32[512,512]{1,0:T(8,128)} %param.4) | copy-start | bytes 3145732
Sparse Core Ops, SparseCore 0:
  9.5 51.9 all-gather.1
  69.7 23.3 reduce-scatter.1
where the time goes:
time: 102 us
  waiting for transfers between devices  76.8 us (75%)
  between operations  13.4 us (13%)
  matrix products  5.71 us (6%)
  other arithmetic  3.07 us (3%)
  local copies, waits for them, and re-layouts  2.64 us (3%)
    all_gather x1, waiting for transfers between devices, per_device(): gathered = lax.all_gather(right_factor, 'row', axis=0, tiled=True)  52.5 us
    reduce_scatter x1, waiting for transfers between devices, per_device(): shared = lax.psum_scatter(total, 'layer', scatter_dimension=1, tiled=True)  23.5 us
    dot_general x1, matrix products, per_device(): jnp.einsum('tak,tsbk->tsab', left_tiles, picked, precision=lax.Precision....  3.43 us
    gather x1, local copies, waits for them, and re-layouts, per_device(): picked = right_tiles[holder]  2.36 us
    dot_general x1, matrix products, per_device(): jnp.einsum('tsab,tsbk->tak', residue, picked, precision=lax.Precision.HIG...  2.28 us
  transfers between devices with their start and end apart: 2, of which 2 were waited for; matrix products, arithmetic and copies ran while one was open for 2% of the time, Pallas kernels for 0%

commit v1 on v0

v1 whole, which is shorter than its diff:
```python
import functools

import jax
import jax.numpy as jnp
from jax import lax
from jax.experimental import pallas as pl
from jax.experimental.pallas import tpu as pltpu
from jax.sharding import PartitionSpec as P

shrink_rate = 0.1
MESH = pl.DeviceIdType.MESH
F32 = jnp.float32
BF16 = jnp.bfloat16


def place_of(index, count):
    odd = index % 2
    return (1 - odd) * (index // 2) + odd * (count - 1 - index // 2)


def index_at(place, count):
    back = place // (count // 2)
    return (1 - back) * (2 * place) + back * (2 * (count - 1 - place) + 1)


def loop(low, high, body):
    if high - low <= 4:
        for step in range(low, high):
            body(step)
    else:

        @pl.loop(low, high)
        def _(step):
            body(step)


def split(value):
    high = value.astype(BF16)
    return high, (value - high.astype(F32)).astype(BF16)


def product(a_pair, b_pair, dims):
    dot = functools.partial(
        lax.dot_general, dimension_numbers=(dims, ((), ())), preferred_element_type=F32
    )
    return dot(a_pair[0], b_pair[0]) + (dot(a_pair[0], b_pair[1]) + dot(a_pair[1], b_pair[0]))


def kernel(
    count, layers, left_hbm, right_hbm, columns, labels_hbm, out,
    tiles, left, left_high, left_low, labels, total, from_core, to_side, from_side,
    local_sem, ring_send, ring_recv, core_send, core_recv, side_send, side_recv,
):
    row, layer = lax.axis_index("row"), lax.axis_index("layer")
    half = count // 2
    size, width = tiles.shape[1], tiles.shape[2]
    trows, slots = labels.shape[0], labels.shape[1]
    part = width // layers
    chunk = size // 2
    sides = layers // 2
    place = place_of(row, count)
    ahead = index_at((place + 1) % count, count)
    behind = index_at((place + count - 1) % count, count)
    core = layer % 2
    side = layer // 2
    twin = side * 2 + (1 - core)
    side_layer = [((side + d) % sides) * 2 + core for d in range(sides)]

    barrier = pltpu.get_barrier_semaphore()
    partners = [(ahead, layer), (behind, layer), (row, twin)]
    partners += [(row, side_layer[d]) for d in range(1, sides)]
    for partner in partners:
        pl.semaphore_signal(barrier, inc=1, device_id=partner, device_id_type=MESH)

    copies = [
        pltpu.make_async_copy(right_hbm, tiles.at[0], local_sem.at[0]),
        pltpu.make_async_copy(left_hbm, left, local_sem.at[1]),
        pltpu.make_async_copy(labels_hbm, labels, local_sem.at[2]),
    ]
    for copy in copies:
        copy.start()
    copies[0].wait()
    pl.semaphore_wait(barrier, len(partners))

    def hop(direction, step, piece):
        if direction == 0:
            source, target, device = step, step + 1, ahead
        else:
            source, target, device = (count - step) % count, count - step - 1, behind
        rows = pl.ds(piece * chunk, chunk)
        return pltpu.make_async_remote_copy(
            src_ref=tiles.at[source, rows],
            dst_ref=tiles.at[target, rows],
            send_sem=ring_send.at[direction, step, piece],
            recv_sem=ring_recv.at[direction, step, piece],
            device_id=(device, layer),
            device_id_type=MESH,
        )

    every = [(0, 0), (1, 1), (0, 1), (1, 0)]

    def moves(last):
        return every[:2] if last else every

    def send(step, chosen):
        for direction, piece in chosen:
            hop(direction, step, piece).start()

    def holder(slot):
        return index_at((place + count - slot) % count, count) * layers + layer

    def residue_of(scores, slot, t):
        tile = holder(slot)
        listed = jnp.zeros((), F32)
        target = jnp.zeros((size, size), F32)
        for s in range(slots):
            match = (columns[t, s] == tile).astype(F32)
            listed = listed + match
            target = target + match * labels[t, s].astype(F32)
        return jax.nn.sigmoid(scores) * listed - target

    def add_tiles(chosen, first):
        value = jnp.concatenate([tiles[slot] for slot in chosen], axis=0)
        right_pair = split(value)
        scores = product((left_high[...], left_low[...]), right_pair, ((1,), (1,)))
        residue = jnp.concatenate(
            [
                jnp.concatenate(
                    [
                        residue_of(
                            scores[t * size:(t + 1) * size, i * size:(i + 1) * size], slot, t
                        )
                        for i, slot in enumerate(chosen)
                    ],
                    axis=1,
                )
                for t in range(trows)
            ],
            axis=0,
        )
        term = product(split(residue), right_pair, ((1,), (0,)))
        for m in range(layers):
            columns_of = term[:, m * part:(m + 1) * part]
            total[m] = columns_of if first else total[m] + columns_of

    send(0, moves(half == 1))
    copies[1].wait()
    high, low = split(left[...])
    left_high[...] = high
    left_low[...] = low
    copies[2].wait()
    add_tiles([0], True)

    def middle(step, last):
        order = moves(last)
        for direction, piece in every:
            hop(direction, step - 1, piece).wait_recv()
            if (direction, piece) in order:
                hop(direction, step, piece).start()
        add_tiles([step, count - step], False)

    loop(1, half - 1, lambda step: middle(step, False))
    if half > 1:
        middle(half - 1, True)
    for direction, piece in moves(True):
        hop(direction, half - 1, piece).wait_recv()
    add_tiles([half], False)

    def core_copy(d):
        return pltpu.make_async_remote_copy(
            src_ref=total.at[((side + d) % sides) * 2 + (1 - core)],
            dst_ref=from_core.at[d],
            send_sem=core_send.at[d],
            recv_sem=core_recv.at[d],
            device_id=(row, twin),
            device_id_type=MESH,
        )

    def side_copy(d):
        return pltpu.make_async_remote_copy(
            src_ref=to_side.at[d - 1],
            dst_ref=from_side.at[d - 1],
            send_sem=side_send.at[d - 1],
            recv_sem=side_recv.at[d - 1],
            device_id=(row, side_layer[d]),
            device_id_type=MESH,
        )

    away = list(range(1, sides)) + [0]
    for d in away:
        core_copy(d).start()
    for d in away:
        core_copy(d).wait_recv()
        own = total[side_layer[d]] + from_core[d]
        if d:
            to_side[d - 1] = own
            side_copy(d).start()
        else:
            out[...] = own + shrink_rate * left[:, pl.ds(pl.multiple_of(layer * part, part), part)]
    for d in range(1, sides):
        side_copy(d).wait_recv()
        out[...] += from_side[d - 1]

    for d in range(1, sides):
        side_copy(d).wait_send()
    for d in away:
        core_copy(d).wait_send()

    def drain(step):
        for direction, piece in every:
            hop(direction, step, piece).wait_send()

    loop(0, half - 1, drain)
    for direction, piece in moves(True):
        hop(direction, half - 1, piece).wait_send()


def per_device(left_factor, right_factor, block_columns, labels):
    count, layers = lax.axis_size("row"), lax.axis_size("layer")
    size, width = right_factor.shape
    rows = left_factor.shape[0]
    part, half, sides = width // layers, count // 2, layers // 2
    dma = pltpu.SemaphoreType.DMA
    return pl.pallas_call(
        functools.partial(kernel, count, layers),
        out_shape=jax.ShapeDtypeStruct((rows, part), F32),
        in_specs=[
            pl.BlockSpec(memory_space=pl.ANY),
            pl.BlockSpec(memory_space=pl.ANY),
            pl.BlockSpec(memory_space=pltpu.SMEM),
            pl.BlockSpec(memory_space=pl.ANY),
        ],
        out_specs=pl.BlockSpec(memory_space=pltpu.VMEM),
        scratch_shapes=[
            pltpu.VMEM((count, size, width), F32),
            pltpu.VMEM((rows, width), F32),
            pltpu.VMEM((rows, width), BF16),
            pltpu.VMEM((rows, width), BF16),
            pltpu.VMEM(labels.shape, jnp.int32),
            pltpu.VMEM((layers, rows, part), F32),
            pltpu.VMEM((sides, rows, part), F32),
            pltpu.VMEM((max(sides - 1, 1), rows, part), F32),
            pltpu.VMEM((max(sides - 1, 1), rows, part), F32),
            dma((3,)),
            dma((2, half, 2)),
            dma((2, half, 2)),
            dma((sides,)),
            dma((sides,)),
            dma((max(sides - 1, 1),)),
            dma((max(sides - 1, 1),)),
        ],
        compiler_params=pltpu.CompilerParams(
            collective_id=0, has_side_effects=True, vmem_limit_bytes=56 * 1024 * 1024
        ),
        cost_estimate=pl.CostEstimate(
            flops=12 * rows * width * size * count,
            bytes_accessed=4 * (rows * width + count * size * width + labels.size + rows * part),
            transcendentals=rows * size * count,
        ),
    )(left_factor, right_factor, block_columns, labels)


def solution(mesh):
    in_specs = (
        P("row", None),
        P(("row", "layer"), None),
        P("row", "layer"),
        P("row", "layer", None, None),
    )
    out_specs = P("row", "layer")
    return jax.shard_map(
        per_device, mesh=mesh, in_specs=in_specs, out_specs=out_specs, check_vma=False
    )
```

time: 102 us -> 39.8 us (0.39)
  waiting for transfers between devices: 76.8 us -> 0 us
  Pallas kernels: 0 us -> 36.4 us
  between operations: 13.4 us -> 0.01 us
  matrix products: 5.71 us -> 0 us
  other arithmetic: 3.07 us -> 0 us
    all_gather x1 -> x0, waiting for transfers between devices: 52.5 us -> none  [per_device(): gathered = lax.all_gather(right_factor, 'row', axis=0, tiled=True)]
    pallas_call x0 -> x1, Pallas kernels: none -> 36.4 us  [per_device(): pl.pallas_call(functools.partial(kernel, count, layers), out_shape=jax.Sh...]
    reduce_scatter x1 -> x0, waiting for transfers between devices: 23.5 us -> none  [per_device(): shared = lax.psum_scatter(total, 'layer', scatter_dimension=1, tiled=True)]
    dot_general x2 -> x0, matrix products: 5.71 us -> none  [the longest x1 3.43 us: per_device(): jnp.einsum('tak,tsbk->tsab', left_tiles, picked, precision=lax.Precision....]
    unnamed x2, local copies, waits for them, and re-layouts: 0.01 us -> 3.01 us
    gather x1 -> x0, local copies, waits for them, and re-layouts: 2.36 us -> none  [per_device(): picked = right_tiles[holder]]
    add x1 -> x0, other arithmetic: 1.7 us -> none  [per_device(): return shared + shrink_rate * own_part]
  transfers between devices with their start and end apart: 2 -> 0, of which waited for: 2 -> 0; matrix products, arithmetic and copies ran while one was open for 2% -> 0% of each run, Pallas kernels for 0% -> 0%
where the time goes in v1:
time: 39.8 us; the launch traced here: 39.4 us
  Pallas kernels  36.4 us (91%)
  local copies, waits for them, and re-layouts  3.01 us (8%)
    pallas_call x1, Pallas kernels, per_device(): pl.pallas_call(functools.partial(kernel, count, layers), out_shape=jax.Sh...  36.4 us
    unnamed x2, local copies, waits for them, and re-layouts  3.01 us

profile of v1, /device:TPU:0, one launch (start us, length us, event | category | flops | bytes accessed | tf_op | source)
XLA Modules:
  0.0 39.4 jit_solution(2639800879209459606)
XLA Ops:
  0.0 1.3 %copy.5.columns = s32[4,2]{1,0:T(4,128)} copy(s32[4,2]{0,1:T(2,128)} %param.6) | data formatting | bytes 64 | tf_op args[2]
  1.3 36.4 %shard_map.46 = f32[512,128]{1,0:T(8,128)} custom-call(f32[512,512]{1,0:T(8,128)} %left_hbm.1, f32[128,512]{1,0:T(8,128)} %right_hbm.1, s32[4,2]{1,0:T(4,128)} %copy.5.columns, s32[4,2,128,128]{3,2,1,0:T(8,128)} %labels_hbm.1), custom_call_target="tpu_custom_call" | custom-call | flops 3221225472 | bytes 3932160 | tf_op jit(solution)/shard_map/pallas_call | solution.py:224
  37.7 1.7 %copy.7 = f32[512,128]{1,0:T(8,128)} copy(f32[512,128]{1,0:T(8,128)} %shard_map.46) | data formatting | bytes 524288

commit v2 on v1

--- a/solution.py
+++ b/solution.py
@@ -8,6 +8,8 @@
 from jax.sharding import PartitionSpec as P
 
 shrink_rate = 0.1
+pieces = 2
+stride = 1
 MESH = pl.DeviceIdType.MESH
 F32 = jnp.float32
 BF16 = jnp.bfloat16
@@ -56,7 +58,7 @@
     size, width = tiles.shape[1], tiles.shape[2]
     trows, slots = labels.shape[0], labels.shape[1]
     part = width // layers
-    chunk = size // 2
+    chunk = size // pieces
     sides = layers // 2
     place = place_of(row, count)
     ahead = index_at((place + 1) % count, count)
@@ -88,6 +90,7 @@
         else:
             source, target, device = (count - step) % count, count - step - 1, behind
         rows = pl.ds(piece * chunk, chunk)
+        own = isinstance(step, int) and step == 0
         return pltpu.make_async_remote_copy(
             src_ref=tiles.at[source, rows],
             dst_ref=tiles.at[target, rows],
@@ -97,10 +100,10 @@
             device_id_type=MESH,
         )
 
-    every = [(0, 0), (1, 1), (0, 1), (1, 0)]
+    every = [(d, (pieces - 1 - i) if d else i) for i in range(pieces) for d in range(2)]
 
     def moves(last):
-        return every[:2] if last else every
+        return every[:pieces] if last else every
 
     def send(step, chosen):
         for direction, piece in chosen:
@@ -114,34 +117,38 @@
         listed = jnp.zeros((), F32)
         target = jnp.zeros((size, size), F32)
         for s in range(slots):
-            match = (columns[t, s] == tile).astype(F32)
+            match = (columns[s, t] == tile).astype(F32)
             listed = listed + match
             target = target + match * labels[t, s].astype(F32)
         return jax.nn.sigmoid(scores) * listed - target
 
-    def add_tiles(chosen, first):
-        value = jnp.concatenate([tiles[slot] for slot in chosen], axis=0)
-        right_pair = split(value)
-        scores = product((left_high[...], left_low[...]), right_pair, ((1,), (1,)))
+    def pair_of(chosen):
+        return split(jnp.concatenate([tiles[slot] for slot in chosen], axis=0))
+
+    def add_tiles(chosen, right_pair, low, high, first=False):
+        rows = slice(low * size, high * size)
+        scores = product((left_high[rows], left_low[rows]), right_pair, ((1,), (1,)))
         residue = jnp.concatenate(
             [
                 jnp.concatenate(
                     [
                         residue_of(
-                            scores[t * size:(t + 1) * size, i * size:(i + 1) * size], slot, t
+                            scores[(t - low) * size:(t - low + 1) * size, i * size:(i + 1) * size],
+                            slot,
+                            t,
                         )
                         for i, slot in enumerate(chosen)
                     ],
                     axis=1,
                 )
-                for t in range(trows)
+                for t in range(low, high)
             ],
             axis=0,
         )
         term = product(split(residue), right_pair, ((1,), (0,)))
         for m in range(layers):
             columns_of = term[:, m * part:(m + 1) * part]
-            total[m] = columns_of if first else total[m] + columns_of
+            total[m, rows] = columns_of if first else total[m, rows] + columns_of
 
     send(0, moves(half == 1))
     copies[1].wait()
@@ -149,7 +156,7 @@
     left_high[...] = high
     left_low[...] = low
     copies[2].wait()
-    add_tiles([0], True)
+    add_tiles([0], pair_of([0]), 0, trows, True)
 
     def middle(step, last):
         order = moves(last)
@@ -157,60 +164,83 @@
             hop(direction, step - 1, piece).wait_recv()
             if (direction, piece) in order:
                 hop(direction, step, piece).start()
-        add_tiles([step, count - step], False)
+        chosen = [step, count - step]
+        add_tiles(chosen, pair_of(chosen), 0, trows)
 
     loop(1, half - 1, lambda step: middle(step, False))
     if half > 1:
         middle(half - 1, True)
     for direction, piece in moves(True):
         hop(direction, half - 1, piece).wait_recv()
-    add_tiles([half], False)
-
-    def core_copy(d):
+
+    def group_rows(g):
+        return pl.ds(g * size, size)
+
+    def core_copy(d, g):
         return pltpu.make_async_remote_copy(
-            src_ref=total.at[((side + d) % sides) * 2 + (1 - core)],
-            dst_ref=from_core.at[d],
-            send_sem=core_send.at[d],
-            recv_sem=core_recv.at[d],
+            src_ref=total.at[((side + d) % sides) * 2 + (1 - core), group_rows(g)],
+            dst_ref=from_core.at[d, group_rows(g)],
+            send_sem=core_send.at[d, g],
+            recv_sem=core_recv.at[d, g],
             device_id=(row, twin),
             device_id_type=MESH,
         )
 
-    def side_copy(d):
+    def side_copy(d, g):
         return pltpu.make_async_remote_copy(
-            src_ref=to_side.at[d - 1],
-            dst_ref=from_side.at[d - 1],
-            send_sem=side_send.at[d - 1],
-            recv_sem=side_recv.at[d - 1],
+            src_ref=to_side.at[d - 1, group_rows(g)],
+            dst_ref=from_side.at[d - 1, group_rows(g)],
+            send_sem=side_send.at[d - 1, g],
+            recv_sem=side_recv.at[d - 1, g],
             device_id=(row, side_layer[d]),
             device_id_type=MESH,
         )
 
-    away = list(range(1, sides)) + [0]
-    for d in away:
-        core_copy(d).start()
-    for d in away:
-        core_copy(d).wait_recv()
-        own = total[side_layer[d]] + from_core[d]
-        if d:
-            to_side[d - 1] = own
-            side_copy(d).start()
-        else:
-            out[...] = own + shrink_rate * left[:, pl.ds(pl.multiple_of(layer * part, part), part)]
-    for d in range(1, sides):
-        side_copy(d).wait_recv()
-        out[...] += from_side[d - 1]
-
-    for d in range(1, sides):
-        side_copy(d).wait_send()
-    for d in away:
-        core_copy(d).wait_send()
+    def pass_on(g):
+        rows = group_rows(g)
+        for d in range(1, sides):
+            core_copy(d, g).wait_recv()
+            to_side[d - 1, rows] = total[side_layer[d], rows] + from_core[d, rows]
+            side_copy(d, g).start()
+
+    last_pair = pair_of([half])
+    for low in range(0, trows, stride):
+        groups = range(low, min(low + stride, trows))
+        add_tiles([half], last_pair, low, groups[-1] + 1)
+        for d in range(1, sides):
+            for g in groups:
+                core_copy(d, g).start()
+        if low:
+            for g in range(low - stride, low):
+                pass_on(g)
+    for g in groups:
+        pass_on(g)
+    for g in range(trows):
+        core_copy(0, g).start()
+    own_part = pl.ds(pl.multiple_of(layer * part, part), part)
+    for g in range(trows):
+        rows = group_rows(g)
+        core_copy(0, g).wait_recv()
+        out[rows] = total[layer, rows] + from_core[0, rows] + shrink_rate * left[rows, own_part]
+    for g in range(trows):
+        rows = group_rows(g)
+        for d in range(1, sides):
+            side_copy(d, g).wait_recv()
+            out[rows] += from_side[d - 1, rows]
+
+    for g in range(trows):
+        for d in range(1, sides):
+            side_copy(d, g).wait_send()
+        for d in range(sides):
+            core_copy(d, g).wait_send()
 
     def drain(step):
         for direction, piece in every:
             hop(direction, step, piece).wait_send()
 
-    loop(0, half - 1, drain)
+    if half > 1:
+        drain(0)
+    loop(1, half - 1, drain)
     for direction, piece in moves(True):
         hop(direction, half - 1, piece).wait_send()
 
@@ -219,11 +249,12 @@
     count, layers = lax.axis_size("row"), lax.axis_size("layer")
     size, width = right_factor.shape
     rows = left_factor.shape[0]
+    trows = labels.shape[0]
     part, half, sides = width // layers, count // 2, layers // 2
     dma = pltpu.SemaphoreType.DMA
     return pl.pallas_call(
         functools.partial(kernel, count, layers),
-        out_shape=jax.ShapeDtypeStruct((rows, part), F32),
+        out_shape=pltpu.VMEM((rows, part), F32),
         in_specs=[
             pl.BlockSpec(memory_space=pl.ANY),
             pl.BlockSpec(memory_space=pl.ANY),
@@ -242,12 +273,12 @@
             pltpu.VMEM((max(sides - 1, 1), rows, part), F32),
             pltpu.VMEM((max(sides - 1, 1), rows, part), F32),
             dma((3,)),
-            dma((2, half, 2)),
-            dma((2, half, 2)),
-            dma((sides,)),
-            dma((sides,)),
-            dma((max(sides - 1, 1),)),
-            dma((max(sides - 1, 1),)),
+            dma((2, half, pieces)),
+            dma((2, half, pieces)),
+            dma((sides, trows)),
+            dma((sides, trows)),
+            dma((max(sides - 1, 1), trows)),
+            dma((max(sides - 1, 1), trows)),
         ],
         compiler_params=pltpu.CompilerParams(
             collective_id=0, has_side_effects=True, vmem_limit_bytes=56 * 1024 * 1024
@@ -257,7 +288,7 @@
             bytes_accessed=4 * (rows * width + count * size * width + labels.size + rows * part),
             transcendentals=rows * size * count,
         ),
-    )(left_factor, right_factor, block_columns, labels)
+    )(left_factor, right_factor, block_columns.T, labels)
 
 
 def solution(mesh):

time: 39.8 us -> 36.9 us (0.927)
  local copies, waits for them, and re-layouts: 3.01 us -> 0.71 us
  Pallas kernels: 36.4 us -> 36 us
    unnamed x2 -> x1, local copies, waits for them, and re-layouts: 3.01 us -> 0.71 us
where the time goes in v2:
time: 36.9 us; the launch traced here: 36.7 us
  Pallas kernels  36 us (98%)
  local copies, waits for them, and re-layouts  0.71 us (2%)
    pallas_call x1, Pallas kernels, per_device(): pl.pallas_call(functools.partial(kernel, count, layers), out_shape=pltpu....  36 us

profile of v2, /device:TPU:0, one launch (start us, length us, event | category | flops | bytes accessed | tf_op | source)
XLA Modules:
  0.0 36.7 jit_solution(14936824176118293624)
XLA Ops:
  0.0 36.0 %shard_map.46 = f32[512,128]{1,0:T(8,128)S(1)} custom-call(f32[512,512]{1,0:T(8,128)} %left_hbm.1, f32[128,512]{1,0:T(8,128)} %right_hbm.1, s32[2,4]{1,0:T(2,128)} %bitcast.1, s32[4,2,128,128]{3,2,1,0:T(8,128)} %labels_hbm.1), custom_call_target="tpu_custom_call" | custom-call | flops 3221225472 | bytes 3932160 | tf_op jit(solution)/shard_map/pallas_call | solution.py:255
  36.0 0.7 %copy.6 = f32[512,128]{1,0:T(8,128)} copy(f32[512,128]{1,0:T(8,128)S(1)} %shard_map.46) | data formatting | bytes 524288

commit v3 on v2

--- a/solution.py
+++ b/solution.py
@@ -49,8 +49,8 @@
 
 
 def kernel(
-    count, layers, left_hbm, right_hbm, columns, labels_hbm, out,
-    tiles, left, left_high, left_low, labels, total, from_core, to_side, from_side,
+    count, layers, left_hbm, right_hbm, columns_hbm, labels_hbm, out,
+    tiles, left, left_high, left_low, labels, columns, total, from_core, to_side, from_side,
     local_sem, ring_send, ring_recv, core_send, core_recv, side_send, side_recv,
 ):
     row, layer = lax.axis_index("row"), lax.axis_index("layer")
@@ -78,9 +78,9 @@
         pltpu.make_async_copy(right_hbm, tiles.at[0], local_sem.at[0]),
         pltpu.make_async_copy(left_hbm, left, local_sem.at[1]),
         pltpu.make_async_copy(labels_hbm, labels, local_sem.at[2]),
+        pltpu.make_async_copy(columns_hbm, columns, local_sem.at[3]),
     ]
-    for copy in copies:
-        copy.start()
+    copies[0].start()
     copies[0].wait()
     pl.semaphore_wait(barrier, len(partners))
 
@@ -151,11 +151,14 @@
             total[m, rows] = columns_of if first else total[m, rows] + columns_of
 
     send(0, moves(half == 1))
+    for copy in copies[1:]:
+        copy.start()
     copies[1].wait()
     high, low = split(left[...])
     left_high[...] = high
     left_low[...] = low
     copies[2].wait()
+    copies[3].wait()
     add_tiles([0], pair_of([0]), 0, trows, True)
 
     def middle(step, last):
@@ -258,7 +261,7 @@
         in_specs=[
             pl.BlockSpec(memory_space=pl.ANY),
             pl.BlockSpec(memory_space=pl.ANY),
-            pl.BlockSpec(memory_space=pltpu.SMEM),
+            pl.BlockSpec(memory_space=pl.ANY),
             pl.BlockSpec(memory_space=pl.ANY),
         ],
         out_specs=pl.BlockSpec(memory_space=pltpu.VMEM),
@@ -268,11 +271,12 @@
             pltpu.VMEM((rows, width), BF16),
             pltpu.VMEM((rows, width), BF16),
             pltpu.VMEM(labels.shape, jnp.int32),
+            pltpu.SMEM(block_columns.shape[::-1], jnp.int32),
             pltpu.VMEM((layers, rows, part), F32),
             pltpu.VMEM((sides, rows, part), F32),
             pltpu.VMEM((max(sides - 1, 1), rows, part), F32),
             pltpu.VMEM((max(sides - 1, 1), rows, part), F32),
-            dma((3,)),
+            dma((4,)),
             dma((2, half, pieces)),
             dma((2, half, pieces)),
             dma((sides, trows)),

time: 36.9 us -> 36.2 us (0.981)
  Pallas kernels: 36 us -> 35.3 us
    pallas_call x1, Pallas kernels: 36 us -> 35.3 us  [per_device(): pl.pallas_call(functools.partial(kernel, count, layers), out_shape=pltpu....]
where the time goes in v3:
time: 36.2 us; the launch traced here: 36 us
  Pallas kernels  35.3 us (98%)
  local copies, waits for them, and re-layouts  0.71 us (2%)
    pallas_call x1, Pallas kernels, per_device(): pl.pallas_call(functools.partial(kernel, count, layers), out_shape=pltpu....  35.3 us

profile of v3, /device:TPU:0, one launch (start us, length us, event | category | flops | bytes accessed | tf_op | source)
XLA Modules:
  0.0 36.0 jit_solution(18115684661668233391)
XLA Ops:
  0.0 35.3 %shard_map.46 = f32[512,128]{1,0:T(8,128)S(1)} custom-call(f32[512,512]{1,0:T(8,128)} %left_hbm.1, f32[128,512]{1,0:T(8,128)} %right_hbm.1, s32[2,4]{1,0:T(2,128)} %bitcast.1, s32[4,2,128,128]{3,2,1,0:T(8,128)} %labels_hbm.1), custom_call_target="tpu_custom_call" | custom-call | flops 3221225472 | bytes 3932160 | tf_op jit(solution)/shard_map/pallas_call | solution.py:258
  35.3 0.7 %copy.6 = f32[512,128]{1,0:T(8,128)} copy(f32[512,128]{1,0:T(8,128)S(1)} %shard_map.46) | data formatting | bytes 524288
